TPU v7x, 32 devices: a whole 2x2x4 slice. The times are simulated.
32 devices in a mesh: tx: 2 (over y), ty: 4 (over z), gz: 4 (over x, core).
Axes of the slice: x: 2, y: 2, z: 4, core: 2. Of those that a mesh axis runs over, the one named last changes fastest.
Arguments:
- tracer_in: float32 [100, 256, 256], P('gz', 'ty', 'tx'), may hold values from -6 to 6
- coef_h: float32 [3, 256, 256], P(None, 'ty', 'tx'), may hold values from 0.05 to 0.2
- coef_v: float32 [3, 100], replicated, may hold values from 0.3 to 1
- wet_levels: int32 [256, 256], P('ty', 'tx'), may hold values from 0 to 100
- column_inv: float32 [100, 100], replicated, may hold values from -0.1 to 1
- sec_cell: int32 [2048], P(('tx', 'ty')), may hold values from 0 to 8191
- sec_gate: int32 [2048], P(('tx', 'ty')), may hold values from 0 to 63
- sec_weight: float32 [2048], P(('tx', 'ty')), may hold values from -6 to 6
Outputs:
- tracer_out: float32 [100, 256, 256], P('gz', 'ty', 'tx')
- gate_flux: float32 [64, 100], P(('tx', 'ty'), 'gz')
Inputs may be any that keep to these rules, and one draw needn't show every extreme that they name: `sec_cell`: index of a cell within the tile of the slot.
All inputs are finite; a program needn't handle non-finite values.
Results may differ from a plain program's by a relative error of at most 0.00015.
Values sent between devices are 32-bit elements; how exact they have to be, the bound alone decides.
A program may use at most 64 MiB of HBM per device.

v0:
```python
import jax
import jax.numpy as jnp
from jax import lax
from jax.sharding import PartitionSpec as P

NSUB = 3
G_DEV = 8
HI = lax.Precision.HIGHEST


def extended(block, axis, dim, width):
    count = lax.axis_size(axis)
    forward = [(i, i + 1) for i in range(count - 1)]
    backward = [(target, source) for source, target in forward]
    low = lax.ppermute(
        lax.slice_in_dim(block, block.shape[dim] - width, None, axis=dim), axis, forward
    )
    high = lax.ppermute(lax.slice_in_dim(block, 0, width, axis=dim), axis, backward)
    return jnp.concatenate([low, block, high], axis=dim)


def diffuse(padded, coef_h, coef_v, wet_levels, level_ids):
    centre = padded[:, 1:-1, 1:-1]
    coef_x = coef_h[0][None] * coef_v[0][:, None, None]
    coef_y = coef_h[1][None] * coef_v[1][:, None, None]
    coef_s = coef_h[2][None] * coef_v[2][:, None, None]
    along_x = padded[:, 1:-1, 2:] - 2.0 * centre + padded[:, 1:-1, :-2]
    along_y = padded[:, 2:, 1:-1] - 2.0 * centre + padded[:, :-2, 1:-1]
    cross = padded[:, 2:, 2:] - padded[:, 2:, :-2] - padded[:, :-2, 2:] + padded[:, :-2, :-2]
    wet = (level_ids[:, None, None] < wet_levels[None]).astype(jnp.float32)
    return wet * (centre + coef_x * along_x + coef_y * along_y + 0.25 * coef_s * cross)


def substeps(field, coef_h, coef_v, wet_levels, level_ids):
    for ring in range(1, NSUB + 1):
        inner = coef_h[:, ring:-ring, ring:-ring]
        field = diffuse(field, inner, coef_v, wet_levels[ring:-ring, ring:-ring], level_ids)
    return field


def vertical(field, column_inv, wet_levels, level_ids):
    levels = column_inv.shape[0]
    flat = field.reshape(levels, -1)
    solved = jnp.dot(column_inv.T, flat, precision=HI).reshape(field.shape)
    wet = (level_ids[:, None, None] < wet_levels[None]).astype(jnp.float32)
    return wet * solved


def per_device(tracer_in, coef_h, coef_v, wet_levels, column_inv, sec_cell, sec_gate, sec_weight):
    depth_count = lax.axis_size("gz")
    depth_index = lax.axis_index("gz")
    tiles = lax.axis_size(("tx", "ty"))
    local_levels, rows, width = tracer_in.shape
    levels = local_levels * depth_count
    col_rows = rows // depth_count
    level_ids = depth_index * local_levels + jnp.arange(local_levels, dtype=jnp.int32)
    all_ids = jnp.arange(levels, dtype=jnp.int32)
    coef_depth = lax.dynamic_slice_in_dim(coef_v, depth_index * local_levels, local_levels, 1)
    row_start = depth_index * col_rows
    gate_ids = jnp.arange(G_DEV * tiles, dtype=jnp.int32)
    gate_hot = jnp.where(gate_ids[:, None] == sec_gate[None, :], sec_weight[None, :], 0.0)
    cells = row_start * width + jnp.arange(col_rows * width, dtype=jnp.int32)
    cell_hot = (sec_cell[:, None] == cells[None, :]).astype(jnp.float32)
    gate_cells = jnp.dot(gate_hot, cell_hot, precision=HI)
    rim = 2 * NSUB
    wet_depth = (level_ids[:, None, None] < wet_levels[None]).astype(jnp.float32)
    packed = jnp.concatenate(
        [wet_depth * tracer_in, coef_h, wet_levels[None].astype(jnp.float32)], axis=0
    )
    packed = extended(extended(packed, "tx", 2, rim), "ty", 1, rim)
    field = packed[:local_levels]
    coef_h = packed[local_levels:-1]
    wet_levels = packed[-1].astype(jnp.int32)
    field = substeps(field, coef_h, coef_depth, wet_levels, level_ids)
    tall = col_rows + 2 * NSUB
    sent = jnp.stack(
        [field[:, part * col_rows : part * col_rows + tall, :] for part in range(depth_count)]
    )
    sent = sent.reshape(depth_count, local_levels, -1)
    field = lax.all_to_all(sent, "gz", split_axis=0, concat_axis=0, tiled=True)
    field = field.reshape(levels, tall, -1)
    coef_h = lax.dynamic_slice_in_dim(coef_h, row_start + NSUB, tall, 1)[:, :, NSUB:-NSUB]
    wet_levels = lax.dynamic_slice_in_dim(wet_levels, row_start + NSUB, tall, 0)[:, NSUB:-NSUB]
    field = vertical(field, column_inv, wet_levels, all_ids)
    total = field[:, NSUB:-NSUB, NSUB:-NSUB]
    field = substeps(field, coef_h, coef_v, wet_levels, all_ids)
    field = vertical(field, column_inv, wet_levels[NSUB:-NSUB, NSUB:-NSUB], all_ids)
    total = total + field
    out = lax.all_to_all(field, "gz", split_axis=0, concat_axis=1, tiled=True)
    flux = lax.dot_general(
        gate_cells, total.reshape(levels, -1), (((1,), (1,)), ((), ())), precision=HI
    )
    flux = flux.reshape(tiles, G_DEV, depth_count, local_levels).transpose(0, 2, 1, 3)
    flux = flux.reshape(tiles * depth_count, G_DEV * local_levels)
    flux = lax.all_to_all(flux, ("tx", "ty", "gz"), split_axis=0, concat_axis=0, tiled=True)
    flux = jnp.sum(flux, axis=0).reshape(G_DEV, local_levels)
    return (out, flux)


def solution(mesh):
    in_specs = (
        P("gz", "ty", "tx"),
        P(None, "ty", "tx"),
        P(),
        P("ty", "tx"),
        P(),
        P(("tx", "ty")),
        P(("tx", "ty")),
        P(("tx", "ty")),
    )
    out_specs = (P("gz", "ty", "tx"), P(("tx", "ty"), "gz"))
    return jax.shard_map(
        per_device, mesh=mesh, in_specs=in_specs, out_specs=out_specs, check_vma=False
    )
```

profile of v0, /device:TPU:0, one launch (start us, length us, event | category | flops | bytes accessed | tf_op | source)
XLA Modules:
  0.0 136.1 jit_solution(9009648317094486944)
XLA Ops:
  4.4 4.9 %collective-permute-start = (f32[29,64,6]{1,0,2:T(8,128)S(1)}, f32[29,64,6]{1,0,2:T(8,128)S(1)}, u32[]{:S(2)}, u32[]{:S(2)}) collective-permute-start(f32[29,64,6]{1,0,2:T(8,128)S(1)} %copy.47), channel_id=1, source_target_pairs={{0,16},{1,17},{2,18},{3,19},{4,20},{5,21},{6,22},{7,23},{8,24},{9,... | collective-permute-start | bytes 133640 | tf_op jit(solution)/shard_map/ppermute | solution.py:15
  11.9 4.3 %collective-permute-done.1 = f32[29,64,6]{1,0,2:T(8,128)S(1)} collective-permute-done((f32[29,64,6]{1,0,2:T(8,128)S(1)}, f32[29,64,6]{1,0,2:T(8,128)S(1)}, u32[]{:S(2)}, u32[]{:S(2)}) %collective-permute-start.1) | collective-permute-done | bytes 44576 | tf_op jit(solution)/shard_map/ppermute | solution.py:18
  17.7 3.5 %collective-permute-start.2 = (f32[29,6,140]{2,1,0:T(8,128)}, f32[29,6,140]{2,1,0:T(8,128)S(1)}, u32[]{:S(2)}, u32[]{:S(2)}) collective-permute-start(f32[29,6,140]{2,1,0:T(8,128)} %get-tuple-element.10), channel_id=1, source_target_pairs={{0,4},{4,8},{8,12},{1,5},{5,9},{9,13},{2,6},{6,10},{10,14},{3,7},{... | collective-permute-start | bytes 292328 | tf_op jit(solution)/shard_map/ppermute | solution.py:15
  22.5 2.6 %collective-permute-done.2 = f32[29,6,140]{2,1,0:T(8,128)S(1)} collective-permute-done((f32[29,6,140]{2,1,0:T(8,128)}, f32[29,6,140]{2,1,0:T(8,128)S(1)}, u32[]{:S(2)}, u32[]{:S(2)}) %collective-permute-start.2) | collective-permute-done | bytes 97472 | tf_op jit(solution)/shard_map/ppermute | solution.py:15
  25.1 4.3 %collective-permute-done.3 = f32[29,6,140]{2,1,0:T(8,128)S(1)} collective-permute-done((f32[29,6,140]{2,1,0:T(8,128)}, f32[29,6,140]{2,1,0:T(8,128)S(1)}, u32[]{:S(2)}, u32[]{:S(2)}) %collective-permute-start.3) | collective-permute-done | bytes 97472 | tf_op jit(solution)/shard_map/ppermute | solution.py:18
  39.1 2.6 %pad_maximum_fusion = f32[29,76,140]{2,1,0:T(8,128)S(1)} fusion(f32[29,6,140]{2,1,0:T(8,128)} %copy-done.5, f32[29,64,6]{2,1,0:T(8,128)} %copy-done.3, f32[1,64,128]{2,1,0:T(8,128)S(1)} %convert_bitcast_fusion, f32[3,64,128]{2,1,0:T(8,128)S(1)} %copy-done.8, f32[25,64,128]{2,1,0:T(8,128)S(1)} %compare_select_fusion, f32[29,64,6]{2,1,0:T(8,128)} %copy-done.1, ...), kind=kLoop, calls=%fused_computation.2 | loop fusion | flops 1851360 | bytes 2468480 | tf_op jit(solution)/shard_map/concatenate | solution.py:19
  41.7 3.7 %fusion.3 = f32[25,74,138]{2,1,0:T(8,128)S(1)} fusion(f32[29,76,140]{2,1,0:T(8,128)S(1)} %pad_maximum_fusion, f32[25]{0:T(128)S(1)} %get-tuple-element.31, f32[74,138]{1,0:T(8,128)S(1)} %get-tuple-element.9, f32[25]{0:T(128)S(1)} %get-tuple-element.32, f32[74,138]{1,0:T(8,128)S(1)} %maximum_bitcast_fusion.1, f32[25]{0:T(128)S(1)} %get-tuple-element.30, ...), kind=kLoop, calls=%fused_computation.8 | loop fusion | flops 5106000 | bytes 10375792 | tf_op jit(solution)/shard_map/mul | solution.py:31
  46.4 3.3 %fusion.17 = f32[25,72,136]{2,1,0:T(8,128)S(1)} fusion(f32[25,74,138]{2,1,0:T(8,128)S(1)} %fusion.3, f32[25]{0:T(128)S(1)} %get-tuple-element.31, f32[72,136]{1,0:T(8,128)S(1)} %get-tuple-element.7, f32[25]{0:T(128)S(1)} %get-tuple-element.32, f32[72,136]{1,0:T(8,128)S(1)} %maximum_bitcast_fusion.7, f32[25]{0:T(128)S(1)} %get-tuple-element.30, ...), kind=kLoop, calls=%fused_computation.36 | loop fusion | flops 4896000 | bytes 9949072 | tf_op jit(solution)/shard_map/mul | solution.py:31
  50.7 3.3 %fusion.10 = f32[25,70,134]{2,1,0:T(8,128)S(1)} fusion(f32[25,72,136]{2,1,0:T(8,128)S(1)} %fusion.17, f32[25]{0:T(128)S(1)} %get-tuple-element.31, f32[70,134]{1,0:T(8,128)S(1)} %get-tuple-element.5, f32[25]{0:T(128)S(1)} %get-tuple-element.32, f32[70,134]{1,0:T(8,128)S(1)} %maximum_bitcast_fusion.4, f32[25]{0:T(128)S(1)} %get-tuple-element.30, ...), kind=kLoop, calls=%fused_computation.22 | loop fusion | flops 4690000 | bytes 9530480 | tf_op jit(solution)/shard_map/mul | solution.py:31
  56.7 2.1 %stack.16 = f32[1,25,2948]{2,1,0:T(8,128)} reshape(f32[25,22,134]{2,1,0:T(8,128)} %get-tuple-element.15) | data formatting | bytes 589600 | tf_op jit(solution)/shard_map/stack | solution.py:76
  58.7 2.1 %stack.17 = f32[1,25,2948]{2,1,0:T(8,128)} reshape(f32[25,22,134]{2,1,0:T(8,128)} %get-tuple-element.14) | data formatting | bytes 589600 | tf_op jit(solution)/shard_map/stack | solution.py:76
  61.8 2.6 %pad_maximum_fusion.1 = f32[4,25,2948]{2,1,0:T(8,128)} fusion(f32[1,25,2948]{2,1,0:T(8,128)} %stack.18, f32[1,25,2948]{2,1,0:T(8,128)} %stack.17, f32[1,25,2948]{2,1,0:T(8,128)} %stack.16, f32[1,25,2948]{2,1,0:T(8,128)S(1)} %stack.15), kind=kLoop, calls=%fused_computation.47 | loop fusion | flops 884400 | bytes 2358400 | tf_op jit(solution)/shard_map/stack | solution.py:76
  64.4 4.7 %all-to-all-start = ((f32[4,25,2948]{2,1,0:T(8,128)}), f32[4,25,2948]{2,1,0:T(8,128)}, u32[]{:S(2)}, u32[]{:S(2)}) async-start(f32[4,25,2948]{2,1,0:T(8,128)} %pad_maximum_fusion.1), calls=%async_computation | async-start | bytes 3145728 | tf_op jit(solution)/shard_map/all_to_all | solution.py:80
  69.1 1.7 %convolution_bitcast_fusion.2 = f32[8,8,2048,1]{2,1,3,0:T(8,128)} fusion(s32[2048]{0:T(1024)S(1)} %iota_add_fusion, s32[256]{0:T(256)S(1)} %copy-done.13, f32[256]{0:T(256)S(1)} %copy-done.14, s32[256]{0:T(256)S(1)} %copy-done.15), kind=kOutput, calls=%fused_computation.3 | convolution fusion | flops 403210240 | bytes 535552 | tf_op jit(solution)/shard_map/dot_general | solution.py:64
  72.2 16.8 %all-to-all-done = f32[4,25,2948]{2,1,0:T(8,128)} async-done(((f32[4,25,2948]{2,1,0:T(8,128)}), f32[4,25,2948]{2,1,0:T(8,128)}, u32[]{:S(2)}, u32[]{:S(2)}) %all-to-all-start) | async-done | bytes 1179232 | tf_op jit(solution)/shard_map/all_to_all | solution.py:80
  93.1 1.9 %fusion.25 = f32[100,20,132]{0,2,1:T(8,128)S(1)} fusion(f32[100,22,134]{0,2,1:T(8,128)S(1)} %fusion.22, f32[100]{0:T(128)S(1)} %get-tuple-element.28, f32[20,132]{1,0:T(8,128)S(1)} %get-tuple-element.25, f32[100]{0:T(128)S(1)} %get-tuple-element.29, f32[20,132]{1,0:T(8,128)S(1)} %get-tuple-element.26, f32[100]{0:T(128)S(1)} %get-tuple-element.27, ...), kind=kLoop, calls=%fused_computation.53 | loop fusion | flops 5280000 | bytes 10603440 | tf_op jit(solution)/shard_map/mul | solution.py:31
  95.0 1.8 %fusion.32 = f32[100,18,130]{0,2,1:T(8,128)S(1)} fusion(f32[100,20,132]{0,2,1:T(8,128)S(1)} %fusion.25, f32[100]{0:T(128)S(1)} %get-tuple-element.28, f32[18,130]{1,0:T(8,128)S(1)} %get-tuple-element.22, f32[100]{0:T(128)S(1)} %get-tuple-element.29, f32[18,130]{1,0:T(8,128)S(1)} %get-tuple-element.23, f32[100]{0:T(128)S(1)} %get-tuple-element.27, ...), kind=kLoop, calls=%fused_computation.68 | loop fusion | flops 4680000 | bytes 9398640 | tf_op jit(solution)/shard_map/mul | solution.py:31
  100.8 2.3 %slice_add_fusion.15 = (f32[100,16,128]{0,2,1:T(8,128)}, f32[100,16,128]{0,2,1:T(8,128)S(1)}) fusion(f32[100,22,134]{0,2,1:T(8,128)S(1)} %fusion.22, f32[100,16,128]{0,2,1:T(8,128)} %bitcast.81, s32[16,128]{1,0:T(8,128)S(1)} %slice.443), kind=kLoop, calls=%fused_computation.81 | loop fusion | flops 614400 | bytes 3284992 | tf_op jit(solution)/shard_map/add | solution.py:88
  103.1 1.7 %copy.71 = f32[100,16,128]{2,1,0:T(8,128)S(1)} copy(f32[100,16,128]{0,2,1:T(8,128)} %get-tuple-element.2) | data formatting | bytes 1638400 | tf_op jit(solution)/shard_map/add | solution.py:88
  104.9 3.7 %convolution_bitcast_fusion.3 = f32[8,4,8,25]{3,2,1,0:T(8,128)S(1)} fusion(f32[8,8,2048,1]{2,1,3,0:T(8,128)} %convolution_bitcast_fusion.2, f32[4,25,2048,1]{2,1,0,3:T(8,128)S(1)} %reshape.67), kind=kOutput, calls=%fused_computation.80 | convolution fusion | flops 157286400 | bytes 1369088 | tf_op jit(solution)/shard_map/dot_general | solution.py:90
  109.4 2.9 %all-to-all-start.2 = ((f32[32,1,200]{2,1,0:T(1,128)}), f32[32,1,200]{2,1,0:T(1,128)S(1)}, u32[]{:S(2)}, u32[]{:S(2)}) async-start(f32[32,1,200]{2,1,0:T(1,128)} %all_to_all.29), calls=%async_computation.2 | async-start | bytes 65536 | tf_op jit(solution)/shard_map/all_to_all | solution.py:95
  113.6 5.9 %all-to-all-done.2 = f32[32,1,200]{2,1,0:T(1,128)S(1)} async-done(((f32[32,1,200]{2,1,0:T(1,128)}), f32[32,1,200]{2,1,0:T(1,128)S(1)}, u32[]{:S(2)}, u32[]{:S(2)}) %all-to-all-start.2) | async-done | bytes 25632 | tf_op jit(solution)/shard_map/all_to_all | solution.py:95
  119.6 3.5 %all-to-all-start.1 = ((f32[100,16,128]{2,1,0:T(8,128)}), f32[100,16,128]{2,1,0:T(8,128)S(1)}, u32[]{:S(2)}, u32[]{:S(2)}) async-start(f32[100,16,128]{2,1,0:T(8,128)} %copy.69), calls=%async_computation.1 | async-start | bytes 1638400 | tf_op jit(solution)/shard_map/all_to_all | solution.py:89
  123.8 11.2 %all-to-all-done.1 = f32[100,16,128]{2,1,0:T(8,128)S(1)} async-done(((f32[100,16,128]{2,1,0:T(8,128)}), f32[100,16,128]{2,1,0:T(8,128)S(1)}, u32[]{:S(2)}, u32[]{:S(2)}) %all-to-all-start.1) | async-done | bytes 819232 | tf_op jit(solution)/shard_map/all_to_all | solution.py:89
  (89 shorter events, 37.6 us)
Async XLA Ops:
  0.6 89.9 %copy-start = (f32[100,100]{1,0:T(8,128)S(1)}, f32[100,100]{1,0:T(8,128)}, u32[]{:S(2)}) copy-start(f32[100,100]{1,0:T(8,128)} %param.12) | copy-start | bytes 120004
  4.0 7.0 %copy-start.12 = (f32[3,100]{1,0:T(4,128)S(1)}, f32[3,100]{1,0:T(4,128)}, u32[]{:S(2)}) copy-start(f32[3,100]{1,0:T(4,128)} %param.10) | copy-start | bytes 3604
  4.0 12.6 %copy-start.7 = (f32[3,64,128]{2,1,0:T(8,128)S(1)}, f32[3,64,128]{2,1,0:T(8,128)}, u32[]{:S(2)}) copy-start(f32[3,64,128]{2,1,0:T(8,128)} %param.9) | copy-start | bytes 294916
  4.4 7.1 %collective-permute-start = (f32[29,64,6]{1,0,2:T(8,128)S(1)}, f32[29,64,6]{1,0,2:T(8,128)S(1)}, u32[]{:S(2)}, u32[]{:S(2)}) collective-permute-start(f32[29,64,6]{1,0,2:T(8,128)S(1)} %copy.47), channel_id=1, source_target_pairs={{0,16},{1,17},{2,18},{3,19},{4,20},{5,21},{6,22},{7,23},{8,24},{9,... | collective-permute-start | bytes 133640 | tf_op jit(solution)/shard_map/ppermute | solution.py:15
  9.7 6.5 %collective-permute-start.1 = (f32[29,64,6]{1,0,2:T(8,128)S(1)}, f32[29,64,6]{1,0,2:T(8,128)S(1)}, u32[]{:S(2)}, u32[]{:S(2)}) collective-permute-start(f32[29,64,6]{1,0,2:T(8,128)S(1)} %copy.48), channel_id=1, source_target_pairs={{16,0},{17,1},{18,2},{19,3},{20,4},{21,5},{22,6},{23,7},{24,8},{25... | collective-permute-start | bytes 133640 | tf_op jit(solution)/shard_map/ppermute | solution.py:18
  11.9 26.3 %copy-start.1 = (f32[29,64,6]{2,1,0:T(8,128)}, f32[29,64,6]{2,1,0:T(8,128)S(1)}, u32[]{:S(2)}) copy-start(f32[29,64,6]{2,1,0:T(8,128)S(1)} %copy.49) | copy-start | bytes 133636
  16.6 21.6 %copy-start.3 = (f32[29,64,6]{2,1,0:T(8,128)}, f32[29,64,6]{2,1,0:T(8,128)S(1)}, u32[]{:S(2)}) copy-start(f32[29,64,6]{2,1,0:T(8,128)S(1)} %copy.50) | copy-start | bytes 133636
  17.7 7.4 %collective-permute-start.2 = (f32[29,6,140]{2,1,0:T(8,128)}, f32[29,6,140]{2,1,0:T(8,128)S(1)}, u32[]{:S(2)}, u32[]{:S(2)}) collective-permute-start(f32[29,6,140]{2,1,0:T(8,128)} %get-tuple-element.10), channel_id=1, source_target_pairs={{0,4},{4,8},{8,12},{1,5},{5,9},{9,13},{2,6},{6,10},{10,14},{3,7},{... | collective-permute-start | bytes 292328 | tf_op jit(solution)/shard_map/ppermute | solution.py:15
  21.2 8.2 %collective-permute-start.3 = (f32[29,6,140]{2,1,0:T(8,128)}, f32[29,6,140]{2,1,0:T(8,128)S(1)}, u32[]{:S(2)}, u32[]{:S(2)}) collective-permute-start(f32[29,6,140]{2,1,0:T(8,128)} %get-tuple-element.11), channel_id=1, source_target_pairs={{4,0},{8,4},{12,8},{5,1},{9,5},{13,9},{6,2},{10,6},{14,10},{7,3},{... | collective-permute-start | bytes 292328 | tf_op jit(solution)/shard_map/ppermute | solution.py:18
  29.4 8.8 %copy-start.5 = (f32[29,6,140]{2,1,0:T(8,128)}, f32[29,6,140]{2,1,0:T(8,128)S(1)}, u32[]{:S(2)}) copy-start(f32[29,6,140]{2,1,0:T(8,128)S(1)} %collective-permute-done.3) | copy-start | bytes 292324
  38.2 0.9 copy-start.8
  39.1 2.6 %copy-start.9 = (s32[74,138]{1,0:T(8,128)S(1)}, s32[74,138]{1,0:T(8,128)}, u32[]{:S(2)}) copy-start(s32[74,138]{1,0:T(8,128)} %copy.54) | copy-start | bytes 122548
  41.7 3.7 %copy-start.2 = (f32[29,64,6]{2,1,0:T(8,128)S(1)}, f32[29,64,6]{2,1,0:T(8,128)}, u32[]{:S(2)}) copy-start(f32[29,64,6]{2,1,0:T(8,128)} %copy-done.1) | copy-start | bytes 133636
  41.7 3.7 %copy-start.4 = (f32[29,64,6]{2,1,0:T(8,128)S(1)}, f32[29,64,6]{2,1,0:T(8,128)}, u32[]{:S(2)}) copy-start(f32[29,64,6]{2,1,0:T(8,128)} %copy-done.3) | copy-start | bytes 133636
  41.7 3.7 %copy-start.6 = (f32[29,6,140]{2,1,0:T(8,128)S(1)}, f32[29,6,140]{2,1,0:T(8,128)}, u32[]{:S(2)}) copy-start(f32[29,6,140]{2,1,0:T(8,128)} %copy-done.5) | copy-start | bytes 292324
  45.5 0.9 copy-start.11
  49.8 0.9 copy-start.10
  64.4 4.7 %copy-start.13 = (s32[256]{0:T(256)S(1)}, s32[256]{0:T(256)}, u32[]{:S(2)}) copy-start(s32[256]{0:T(256)} %param.13) | copy-start | bytes 3076
  64.4 4.7 %copy-start.14 = (f32[256]{0:T(256)S(1)}, f32[256]{0:T(256)}, u32[]{:S(2)}) copy-start(f32[256]{0:T(256)} %param.15) | copy-start | bytes 3076
  64.4 4.7 %copy-start.15 = (s32[256]{0:T(256)S(1)}, s32[256]{0:T(256)}, u32[]{:S(2)}) copy-start(s32[256]{0:T(256)} %param.14) | copy-start | bytes 3076
  64.4 24.6 %all-to-all-start = ((f32[4,25,2948]{2,1,0:T(8,128)}), f32[4,25,2948]{2,1,0:T(8,128)}, u32[]{:S(2)}, u32[]{:S(2)}) async-start(f32[4,25,2948]{2,1,0:T(8,128)} %pad_maximum_fusion.1), calls=%async_computation | async-start | bytes 3145728 | tf_op jit(solution)/shard_map/all_to_all | solution.py:80
  109.4 10.2 %all-to-all-start.2 = ((f32[32,1,200]{2,1,0:T(1,128)}), f32[32,1,200]{2,1,0:T(1,128)S(1)}, u32[]{:S(2)}, u32[]{:S(2)}) async-start(f32[32,1,200]{2,1,0:T(1,128)} %all_to_all.29), calls=%async_computation.2 | async-start | bytes 65536 | tf_op jit(solution)/shard_map/all_to_all | solution.py:95
  119.6 15.5 %all-to-all-start.1 = ((f32[100,16,128]{2,1,0:T(8,128)}), f32[100,16,128]{2,1,0:T(8,128)S(1)}, u32[]{:S(2)}, u32[]{:S(2)}) async-start(f32[100,16,128]{2,1,0:T(8,128)} %copy.69), calls=%async_computation.1 | async-start | bytes 1638400 | tf_op jit(solution)/shard_map/all_to_all | solution.py:89
where the time goes:
time: 137 us; the launch traced here: 136 us
  waiting for transfers between devices  45.6 us (33%)
  local copies, waits for them, and re-layouts  30.3 us (22%)
  other arithmetic  29.2 us (21%)
  starting transfers between devices  22 us (16%)
  matrix products  7.83 us (6%)
    all_to_all x1, waiting for transfers between devices, per_device(): field = lax.all_to_all(sent, 'gz', split_axis=0, concat_axis=0, tiled=True)  16.8 us
    mul x6, other arithmetic, diffuse(): wet * (centre + coef_x * along_x + coef_y * along_y + 0.25 * coef_s * cross)  15.5 us
    all_to_all x1, waiting for transfers between devices, per_device(): out = lax.all_to_all(field, 'gz', split_axis=0, concat_axis=1, tiled=True)  11.2 us
    ppermute x2, waiting for transfers between devices, extended(): lax.ppermute(lax.slice_in_dim(block, 0, width, axis=dim), axis, backward)  8.61 us
    ppermute x2, starting transfers between devices, extended(): lax.ppermute(lax.slice_in_dim(block, block.shape[dim] - width, None, axis...  8.36 us
    slice x8, local copies, waits for them, and re-layouts, substeps(): wet_levels[ring:-ring, ring:-ring]  7.11 us
    another operation x4, local copies, waits for them, and re-layouts, per_device(): jnp.stack([field[:, part * col_rows:part * col_rows + tall, :] for part i...  6.45 us
    all_to_all x1, waiting for transfers between devices, per_device(): lax.all_to_all(flux, ('tx', 'ty', 'gz'), split_axis=0, concat_axis=0, til...  5.94 us
  transfers between devices with their start and end apart: 7, of which 7 were waited for; matrix products, arithmetic and copies ran while one was open for 4% of the time, Pallas kernels for 0%

commit v1 on v0

--- a/solution.py
+++ b/solution.py
@@ -6,6 +6,20 @@
 NSUB = 3
 G_DEV = 8
 HI = lax.Precision.HIGHEST
+
+
+def squares_time(m, along_dim, inner_x):
+    n_now, current_block = (m.shape[:along_dim], m.shape[along_dim + 1 :])
+    work_now = m.reshape(*n_now, inner_x, -1, *current_block)
+    return jnp.moveaxis(work_now, along_dim, 0)
+
+
+def _finish_tiles(shard_in, axis_no):
+    shard_in = jnp.moveaxis(shard_in, 0, axis_no)
+    left_arr = shard_in.shape
+    return shard_in.reshape(
+        *left_arr[:axis_no], left_arr[axis_no] * left_arr[axis_no + 1], *left_arr[axis_no + 2 :]
+    )
 
 
 def extended(block, axis, dim, width):
@@ -77,7 +91,20 @@
         [field[:, part * col_rows : part * col_rows + tall, :] for part in range(depth_count)]
     )
     sent = sent.reshape(depth_count, local_levels, -1)
-    field = lax.all_to_all(sent, "gz", split_axis=0, concat_axis=0, tiled=True)
+
+    def make_targets(view, mesh_name, chunk, original):
+        latest = lax.axis_size(mesh_name)
+        frame_out = lax.axis_index(mesh_name)
+        found_now, b_next = (latest, frame_out)
+        w2 = squares_time(view, chunk, found_now)
+        rack = [w2[b_next]]
+        for kk in range(1, found_now):
+            f_now = w2[b_next ^ kk]
+            rack.append(lax.ppermute(f_now, mesh_name, [(no, no ^ kk) for no in range(found_now)]))
+        w2 = jnp.stack(rack)[b_next ^ jnp.arange(found_now)]
+        return _finish_tiles(w2, original)
+
+    field = make_targets(sent, "gz", 0, 0)
     field = field.reshape(levels, tall, -1)
     coef_h = lax.dynamic_slice_in_dim(coef_h, row_start + NSUB, tall, 1)[:, :, NSUB:-NSUB]
     wet_levels = lax.dynamic_slice_in_dim(wet_levels, row_start + NSUB, tall, 0)[:, NSUB:-NSUB]

time: 137 us -> 121 us (0.88)
  local copies, waits for them, and re-layouts: 30.3 us -> 23.9 us
  other arithmetic: 29.2 us -> 24.4 us
  waiting for transfers between devices: 45.6 us -> 41.5 us
    ppermute x0 -> x3, waiting for transfers between devices: none -> 17.7 us  [make_targets(): lax.ppermute(f_now, mesh_name, [(no, no ^ kk) for no in range(found_now)])]
    all_to_all x1 -> x0, waiting for transfers between devices: 16.8 us -> none  [per_device(): field = lax.all_to_all(sent, 'gz', split_axis=0, concat_axis=0, tiled=True)]
    another operation x4 -> x5, local copies, waits for them, and re-layouts: 6.45 us -> 1.09 us  [per_device(): jnp.stack([field[:, part * col_rows:part * col_rows + tall, :] for part i...]
    all_to_all x1 -> x0, starting transfers between devices: 4.65 us -> none  [per_device(): field = lax.all_to_all(sent, 'gz', split_axis=0, concat_axis=0, tiled=True)]
    ppermute x2, waiting for transfers between devices: 8.61 us -> 4.13 us  [extended(): lax.ppermute(lax.slice_in_dim(block, 0, width, axis=dim), axis, backward)]
    another operation x1, other arithmetic: 2.58 us -> 0.12 us  [make_targets(): w2 = jnp.stack(rack)[b_next ^ jnp.arange(found_now)]]
    ppermute x0 -> x3, starting transfers between devices: none -> 1.92 us  [make_targets(): lax.ppermute(f_now, mesh_name, [(no, no ^ kk) for no in range(found_now)])]
    concatenate x1, other arithmetic: 2.55 us -> 0.93 us  [extended(): return jnp.concatenate([low, block, high], axis=dim)]
  transfers between devices with their start and end apart: 7 -> 9, of which waited for: 7 -> 6; matrix products, arithmetic and copies ran while one was open for 4% -> 6% of each run, Pallas kernels for 0% -> 0%
where the time goes in v1:
time: 121 us; the launch traced here: 120 us
  waiting for transfers between devices  41.5 us (34%)
  other arithmetic  24.4 us (20%)
  local copies, waits for them, and re-layouts  23.9 us (20%)
  starting transfers between devices  20.9 us (17%)
  matrix products  7.83 us (6%)
    ppermute x3, waiting for transfers between devices, make_targets(): lax.ppermute(f_now, mesh_name, [(no, no ^ kk) for no in range(found_now)])  17.7 us
    mul x6, other arithmetic, diffuse(): wet * (centre + coef_x * along_x + coef_y * along_y + 0.25 * coef_s * cross)  15.7 us
    all_to_all x1, waiting for transfers between devices, per_device(): out = lax.all_to_all(field, 'gz', split_axis=0, concat_axis=1, tiled=True)  11.2 us
    ppermute x2, starting transfers between devices, extended(): lax.ppermute(lax.slice_in_dim(block, block.shape[dim] - width, None, axis...  9.49 us
    all_to_all x1, waiting for transfers between devices, per_device(): lax.all_to_all(flux, ('tx', 'ty', 'gz'), split_axis=0, concat_axis=0, til...  5.94 us
    slice x8, local copies, waits for them, and re-layouts, substeps(): wet_levels[ring:-ring, ring:-ring]  5.54 us
    ppermute x2, waiting for transfers between devices, extended(): lax.ppermute(lax.slice_in_dim(block, 0, width, axis=dim), axis, backward)  4.13 us
    dot_general x1, matrix products, per_device(): lax.dot_general(gate_cells, total.reshape(levels, -1), (((1,), (1,)), (()...  3.75 us
  transfers between devices with their start and end apart: 9, of which 6 were waited for; matrix products, arithmetic and copies ran while one was open for 6% of the time, Pallas kernels for 0%

profile of v1, /device:TPU:0, one launch (start us, length us, event | category | flops | bytes accessed | tf_op | source)
XLA Modules:
  0.0 119.7 jit_solution(14814619938706143772)
XLA Ops:
  6.1 4.9 %collective-permute-start = (f32[29,64,6]{1,0,2:T(8,128)S(1)}, f32[29,64,6]{1,0,2:T(8,128)S(1)}, u32[]{:S(2)}, u32[]{:S(2)}) collective-permute-start(f32[29,64,6]{1,0,2:T(8,128)S(1)} %copy.47), channel_id=1, source_target_pairs={{0,16},{1,17},{2,18},{3,19},{4,20},{5,21},{6,22},{7,23},{8,24},{9,... | collective-permute-start | bytes 133640 | tf_op jit(solution)/shard_map/ppermute | solution.py:29
  12.3 1.7 %convolution_bitcast_fusion.2 = f32[8,8,2048,1]{2,1,3,0:T(8,128)} fusion(s32[2048]{0:T(1024)S(1)} %iota_add_fusion, s32[256]{0:T(256)S(1)} %copy-done.13, f32[256]{0:T(256)S(1)} %copy-done.14, s32[256]{0:T(256)S(1)} %copy-done.15), kind=kOutput, calls=%fused_computation.4 | convolution fusion | flops 403210240 | bytes 535552 | tf_op jit(solution)/shard_map/dot_general | solution.py:78
  15.1 4.6 %collective-permute-start.2 = (f32[29,6,140]{2,1,0:T(8,128)S(1)}, f32[29,6,140]{2,1,0:T(8,128)S(1)}, u32[]{:S(2)}, u32[]{:S(2)}) collective-permute-start(f32[29,6,140]{2,1,0:T(8,128)S(1)} %get-tuple-element.10), channel_id=1, source_target_pairs={{0,4},{4,8},{8,12},{1,5},{5,9},{9,13},{2,6},{6,10},{10,14},{3,7},{... | collective-permute-start | bytes 292328 | tf_op jit(solution)/shard_map/ppermute | solution.py:29
  19.7 1.3 %collective-permute-start.3 = (f32[29,6,140]{2,1,0:T(8,128)S(1)}, f32[29,6,140]{2,1,0:T(8,128)S(1)}, u32[]{:S(2)}, u32[]{:S(2)}) collective-permute-start(f32[29,6,140]{2,1,0:T(8,128)S(1)} %get-tuple-element.11), channel_id=1, source_target_pairs={{4,0},{8,4},{12,8},{5,1},{9,5},{13,9},{6,2},{10,6},{14,10},{7,3},{... | collective-permute-start | bytes 292328 | tf_op jit(solution)/shard_map/ppermute | solution.py:32
  21.6 2.5 %collective-permute-done.2 = f32[29,6,140]{2,1,0:T(8,128)S(1)} collective-permute-done((f32[29,6,140]{2,1,0:T(8,128)S(1)}, f32[29,6,140]{2,1,0:T(8,128)S(1)}, u32[]{:S(2)}, u32[]{:S(2)}) %collective-permute-start.2) | collective-permute-done | bytes 97472 | tf_op jit(solution)/shard_map/ppermute | solution.py:29
  24.1 4.1 %collective-permute-done.3 = f32[29,6,140]{2,1,0:T(8,128)S(1)} collective-permute-done((f32[29,6,140]{2,1,0:T(8,128)S(1)}, f32[29,6,140]{2,1,0:T(8,128)S(1)}, u32[]{:S(2)}, u32[]{:S(2)}) %collective-permute-start.3) | collective-permute-done | bytes 97472 | tf_op jit(solution)/shard_map/ppermute | solution.py:32
  38.7 3.6 %fusion.3 = f32[25,74,138]{2,1,0:T(8,128)S(1)} fusion(f32[29,76,140]{2,1,0:T(8,128)S(1)} %pad_maximum_fusion, f32[25]{0:T(128)S(1)} %copy-done.10, f32[74,138]{1,0:T(8,128)S(1)} %get-tuple-element.9, f32[25]{0:T(128)S(1)} %copy-done.11, f32[74,138]{1,0:T(8,128)S(1)} %maximum_bitcast_fusion.2, f32[25]{0:T(128)S(1)} %copy-done.9, ...), kind=kLoop, calls=%fused_computation.9 | loop fusion | flops 5106000 | bytes 10375792 | tf_op jit(solution)/shard_map/mul | solution.py:45
  43.4 3.3 %fusion.17 = f32[25,72,136]{2,1,0:T(8,128)S(1)} fusion(f32[25,74,138]{2,1,0:T(8,128)S(1)} %fusion.3, f32[25]{0:T(128)S(1)} %copy-done.10, f32[72,136]{1,0:T(8,128)S(1)} %get-tuple-element.7, f32[25]{0:T(128)S(1)} %copy-done.11, f32[72,136]{1,0:T(8,128)S(1)} %maximum_bitcast_fusion.8, f32[25]{0:T(128)S(1)} %copy-done.9, f32[72,136]{1,0:T(8,128)S(1)} %get-tuple-element.6, ...), kind=kLoop, calls=%fused_computation.37 | loop fusion | flops 4896000 | bytes 9949072 | tf_op jit(solution)/shard_map/mul | solution.py:45
  47.0 3.3 %fusion.10 = f32[25,70,134]{2,1,0:T(8,128)S(1)} fusion(f32[25,72,136]{2,1,0:T(8,128)S(1)} %fusion.17, f32[25]{0:T(128)S(1)} %copy-done.10, f32[70,134]{1,0:T(8,128)S(1)} %get-tuple-element.5, f32[25]{0:T(128)S(1)} %copy-done.11, f32[70,134]{1,0:T(8,128)S(1)} %maximum_bitcast_fusion.5, f32[25]{0:T(128)S(1)} %copy-done.9, f32[70,134]{1,0:T(8,128)S(1)} %get-tuple-element.4, ...), kind=kLoop, calls=%fused_computation.23 | loop fusion | flops 4690000 | bytes 9530480 | tf_op jit(solution)/shard_map/mul | solution.py:45
  51.9 1.6 %collective-permute-start.5 = (f32[1,25,2948]{2,1,0:T(8,128)S(1)}, f32[1,25,2948]{2,1,0:T(8,128)S(1)}, u32[]{:S(2)}, u32[]{:S(2)}) collective-permute-start(f32[1,25,2948]{2,1,0:T(8,128)S(1)} %get-tuple-element.18), channel_id=1, source_target_pairs={{0,2},{1,3},{2,0},{3,1},{4,6},{5,7},{6,4},{7,5},{8,10},{9,11},{10,... | collective-permute-start | bytes 884408 | tf_op jit(solution)/shard_map/ppermute | solution.py:103
  54.1 9.2 %collective-permute-done.6 = f32[1,25,2948]{2,1,0:T(8,128)S(1)} collective-permute-done((f32[1,25,2948]{2,1,0:T(8,128)S(1)}, f32[1,25,2948]{2,1,0:T(8,128)S(1)}, u32[]{:S(2)}, u32[]{:S(2)}) %collective-permute-start.6) | collective-permute-done | bytes 294832 | tf_op jit(solution)/shard_map/ppermute | solution.py:103
  63.3 8.5 %collective-permute-done.5 = f32[1,25,2948]{2,1,0:T(8,128)S(1)} collective-permute-done((f32[1,25,2948]{2,1,0:T(8,128)S(1)}, f32[1,25,2948]{2,1,0:T(8,128)S(1)}, u32[]{:S(2)}, u32[]{:S(2)}) %collective-permute-start.5) | collective-permute-done | bytes 294832 | tf_op jit(solution)/shard_map/ppermute | solution.py:103
  76.1 1.9 %fusion.25 = f32[100,20,132]{0,2,1:T(8,128)S(1)} fusion(f32[100,22,134]{0,2,1:T(8,128)S(1)} %fusion.22, f32[100]{0:T(128)S(1)} %get-tuple-element.32, f32[20,132]{1,0:T(8,128)S(1)} %get-tuple-element.29, f32[100]{0:T(128)S(1)} %copy-done.8, f32[20,132]{1,0:T(8,128)S(1)} %get-tuple-element.30, f32[100]{0:T(128)S(1)} %get-tuple-element.31, ...), kind=kLoop, calls=%fused_computation.54 | loop fusion | flops 5280000 | bytes 10603440 | tf_op jit(solution)/shard_map/mul | solution.py:45
  78.0 1.8 %fusion.32 = f32[100,18,130]{0,2,1:T(8,128)S(1)} fusion(f32[100,20,132]{0,2,1:T(8,128)S(1)} %fusion.25, f32[100]{0:T(128)S(1)} %get-tuple-element.32, f32[18,130]{1,0:T(8,128)S(1)} %get-tuple-element.26, f32[100]{0:T(128)S(1)} %copy-done.8, f32[18,130]{1,0:T(8,128)S(1)} %get-tuple-element.27, f32[100]{0:T(128)S(1)} %get-tuple-element.31, ...), kind=kLoop, calls=%fused_computation.69 | loop fusion | flops 4680000 | bytes 9398640 | tf_op jit(solution)/shard_map/mul | solution.py:45
  79.9 1.7 %fusion.39 = f32[100,16,128]{0,2,1:T(8,128)S(1)} fusion(f32[100,18,130]{0,2,1:T(8,128)S(1)} %fusion.32, f32[100]{0:T(128)S(1)} %get-tuple-element.32, f32[16,128]{1,0:T(8,128)S(1)} %get-tuple-element.24, f32[100]{0:T(128)S(1)} %copy-done.8, f32[16,128]{1,0:T(8,128)S(1)} %get-tuple-element.23, f32[100]{0:T(128)S(1)} %get-tuple-element.31, ...), kind=kLoop, calls=%fused_computation.86 | loop fusion | flops 4096000 | bytes 8225968 | tf_op jit(solution)/shard_map/mul | solution.py:45
  82.7 1.3 %copy.80 = f32[100,2048]{0,1:T(8,128)} copy(f32[100,2048]{1,0:T(8,128)S(1)} %convolution_bitcast_fusion.1) | data formatting | bytes 1638400 | tf_op jit(solution)/shard_map/reshape | solution.py:58
  84.0 2.3 %slice_add_fusion.15 = (f32[100,16,128]{0,2,1:T(8,128)}, f32[100,16,128]{0,2,1:T(8,128)S(1)}) fusion(f32[100,22,134]{0,2,1:T(8,128)S(1)} %fusion.22, f32[100,16,128]{0,2,1:T(8,128)} %bitcast.94, s32[16,128]{1,0:T(8,128)S(1)} %slice.445), kind=kLoop, calls=%fused_computation.82 | loop fusion | flops 614400 | bytes 3284992 | tf_op jit(solution)/shard_map/add | solution.py:115
  86.2 1.7 %copy.71 = f32[100,16,128]{2,1,0:T(8,128)S(1)} copy(f32[100,16,128]{0,2,1:T(8,128)} %get-tuple-element.2) | data formatting | bytes 1638400 | tf_op jit(solution)/shard_map/add | solution.py:115
  88.1 3.7 %convolution_bitcast_fusion.3 = f32[8,4,8,25]{3,2,1,0:T(8,128)S(1)} fusion(f32[8,8,2048,1]{2,1,3,0:T(8,128)} %convolution_bitcast_fusion.2, f32[4,25,2048,1]{2,1,0,3:T(8,128)S(1)} %reshape.93), kind=kOutput, calls=%fused_computation.81 | convolution fusion | flops 157286400 | bytes 1369088 | tf_op jit(solution)/shard_map/dot_general | solution.py:117
  92.6 3.4 %all-to-all-start.1 = ((f32[32,1,200]{2,1,0:T(1,128)}), f32[32,1,200]{2,1,0:T(1,128)S(1)}, u32[]{:S(2)}, u32[]{:S(2)}) async-start(f32[32,1,200]{2,1,0:T(1,128)} %all_to_all.25), calls=%async_computation.1 | async-start | bytes 65536 | tf_op jit(solution)/shard_map/all_to_all | solution.py:122
  96.0 1.3 %copy.69 = f32[100,16,128]{2,1,0:T(8,128)} copy(f32[100,16,128]{0,2,1:T(8,128)S(1)} %get-tuple-element.3) | data formatting | bytes 1638400 | tf_op jit(solution)/shard_map/mul | solution.py:60
  97.3 5.9 %all-to-all-done.1 = f32[32,1,200]{2,1,0:T(1,128)S(1)} async-done(((f32[32,1,200]{2,1,0:T(1,128)}), f32[32,1,200]{2,1,0:T(1,128)S(1)}, u32[]{:S(2)}, u32[]{:S(2)}) %all-to-all-start.1) | async-done | bytes 25632 | tf_op jit(solution)/shard_map/all_to_all | solution.py:122
  103.2 3.5 %all-to-all-start = ((f32[100,16,128]{2,1,0:T(8,128)}), f32[100,16,128]{2,1,0:T(8,128)S(1)}, u32[]{:S(2)}, u32[]{:S(2)}) async-start(f32[100,16,128]{2,1,0:T(8,128)} %copy.69), calls=%async_computation | async-start | bytes 1638400 | tf_op jit(solution)/shard_map/all_to_all | solution.py:116
  107.5 11.2 %all-to-all-done = f32[100,16,128]{2,1,0:T(8,128)S(1)} async-done(((f32[100,16,128]{2,1,0:T(8,128)}), f32[100,16,128]{2,1,0:T(8,128)S(1)}, u32[]{:S(2)}, u32[]{:S(2)}) %all-to-all-start) | async-done | bytes 819232 | tf_op jit(solution)/shard_map/all_to_all | solution.py:116
  (101 shorter events, 30.0 us)
Async XLA Ops:
  0.6 72.2 %copy-start = (f32[100,100]{1,0:T(8,128)S(1)}, f32[100,100]{1,0:T(8,128)}, u32[]{:S(2)}) copy-start(f32[100,100]{1,0:T(8,128)} %param.12) | copy-start | bytes 120004
  4.0 7.0 %copy-start.12 = (f32[3,100]{1,0:T(4,128)S(1)}, f32[3,100]{1,0:T(4,128)}, u32[]{:S(2)}) copy-start(f32[3,100]{1,0:T(4,128)} %param.10) | copy-start | bytes 3604
  4.0 8.3 %copy-start.13 = (s32[256]{0:T(256)S(1)}, s32[256]{0:T(256)}, u32[]{:S(2)}) copy-start(s32[256]{0:T(256)} %param.13) | copy-start | bytes 3076
  4.0 8.3 %copy-start.14 = (f32[256]{0:T(256)S(1)}, f32[256]{0:T(256)}, u32[]{:S(2)}) copy-start(f32[256]{0:T(256)} %param.15) | copy-start | bytes 3076
  4.0 8.2 %copy-start.15 = (s32[256]{0:T(256)S(1)}, s32[256]{0:T(256)}, u32[]{:S(2)}) copy-start(s32[256]{0:T(256)} %param.14) | copy-start | bytes 3076
  4.4 10.0 %collective-permute-start.1 = (f32[29,64,6]{1,0,2:T(8,128)S(1)}, f32[29,64,6]{1,0,2:T(8,128)S(1)}, u32[]{:S(2)}, u32[]{:S(2)}) collective-permute-start(f32[29,64,6]{1,0,2:T(8,128)S(1)} %copy.48), channel_id=1, source_target_pairs={{16,0},{17,1},{18,2},{19,3},{20,4},{21,5},{22,6},{23,7},{24,8},{25... | collective-permute-start | bytes 133640 | tf_op jit(solution)/shard_map/ppermute | solution.py:32
  5.7 9.1 %copy-start.1 = (f32[3,64,128]{2,1,0:T(8,128)S(1)}, f32[3,64,128]{2,1,0:T(8,128)}, u32[]{:S(2)}) copy-start(f32[3,64,128]{2,1,0:T(8,128)} %param.9) | copy-start | bytes 294916
  6.1 7.9 %collective-permute-start = (f32[29,64,6]{1,0,2:T(8,128)S(1)}, f32[29,64,6]{1,0,2:T(8,128)S(1)}, u32[]{:S(2)}, u32[]{:S(2)}) collective-permute-start(f32[29,64,6]{1,0,2:T(8,128)S(1)} %copy.47), channel_id=1, source_target_pairs={{0,16},{1,17},{2,18},{3,19},{4,20},{5,21},{6,22},{7,23},{8,24},{9,... | collective-permute-start | bytes 133640 | tf_op jit(solution)/shard_map/ppermute | solution.py:29
  15.1 9.1 %collective-permute-start.2 = (f32[29,6,140]{2,1,0:T(8,128)S(1)}, f32[29,6,140]{2,1,0:T(8,128)S(1)}, u32[]{:S(2)}, u32[]{:S(2)}) collective-permute-start(f32[29,6,140]{2,1,0:T(8,128)S(1)} %get-tuple-element.10), channel_id=1, source_target_pairs={{0,4},{4,8},{8,12},{1,5},{5,9},{9,13},{2,6},{6,10},{10,14},{3,7},{... | collective-permute-start | bytes 292328 | tf_op jit(solution)/shard_map/ppermute | solution.py:29
  19.7 8.6 %collective-permute-start.3 = (f32[29,6,140]{2,1,0:T(8,128)S(1)}, f32[29,6,140]{2,1,0:T(8,128)S(1)}, u32[]{:S(2)}, u32[]{:S(2)}) collective-permute-start(f32[29,6,140]{2,1,0:T(8,128)S(1)} %get-tuple-element.11), channel_id=1, source_target_pairs={{4,0},{8,4},{12,8},{5,1},{9,5},{13,9},{6,2},{10,6},{14,10},{7,3},{... | collective-permute-start | bytes 292328 | tf_op jit(solution)/shard_map/ppermute | solution.py:32
  28.4 0.6 copy-start.3
  38.0 0.6 copy-start.10
  38.1 0.7 copy-start.11
  42.5 0.9 copy-start.4
  51.6 2.1 %copy-start.2 = (f32[3,76,140]{2,1,0:T(8,128)S(1)}, f32[3,76,140]{2,1,0:T(8,128)}, u32[]{:S(2)}) copy-start(f32[3,76,140]{2,1,0:T(8,128)} %slice.484) | copy-start | bytes 383044
  51.8 11.4 %collective-permute-start.6 = (f32[1,25,2948]{2,1,0:T(8,128)S(1)}, f32[1,25,2948]{2,1,0:T(8,128)S(1)}, u32[]{:S(2)}, u32[]{:S(2)}) collective-permute-start(f32[1,25,2948]{2,1,0:T(8,128)S(1)} %get-tuple-element.17), channel_id=1, source_target_pairs={{0,3},{1,2},{2,1},{3,0},{4,7},{5,6},{6,5},{7,4},{8,11},{9,10},{10,... | collective-permute-start | bytes 884408 | tf_op jit(solution)/shard_map/ppermute | solution.py:103
  51.9 19.8 %collective-permute-start.5 = (f32[1,25,2948]{2,1,0:T(8,128)S(1)}, f32[1,25,2948]{2,1,0:T(8,128)S(1)}, u32[]{:S(2)}, u32[]{:S(2)}) collective-permute-start(f32[1,25,2948]{2,1,0:T(8,128)S(1)} %get-tuple-element.18), channel_id=1, source_target_pairs={{0,2},{1,3},{2,0},{3,1},{4,6},{5,7},{6,4},{7,5},{8,10},{9,11},{10,... | collective-permute-start | bytes 884408 | tf_op jit(solution)/shard_map/ppermute | solution.py:103
  53.5 18.3 %collective-permute-start.4 = (f32[1,25,2948]{2,1,0:T(8,128)S(1)}, f32[1,25,2948]{2,1,0:T(8,128)S(1)}, u32[]{:S(2)}, u32[]{:S(2)}) collective-permute-start(f32[1,25,2948]{2,1,0:T(8,128)S(1)} %get-tuple-element.19), channel_id=1, source_target_pairs={{0,1},{1,0},{2,3},{3,2},{4,5},{5,4},{6,7},{7,6},{8,9},{9,8},{10,11... | collective-permute-start | bytes 884408 | tf_op jit(solution)/shard_map/ppermute | solution.py:103
  74.6 0.7 copy-start.6
  75.3 0.7 copy-start.7
  75.3 0.7 copy-start.8
  76.1 1.9 %copy-start.5 = (s32[18,130]{1,0:T(8,128)S(1)}, s32[18,130]{1,0:T(8,128)}, u32[]{:S(2)}) copy-start(s32[18,130]{1,0:T(8,128)} %slice.446) | copy-start | bytes 28084
  92.6 10.7 %all-to-all-start.1 = ((f32[32,1,200]{2,1,0:T(1,128)}), f32[32,1,200]{2,1,0:T(1,128)S(1)}, u32[]{:S(2)}, u32[]{:S(2)}) async-start(f32[32,1,200]{2,1,0:T(1,128)} %all_to_all.25), calls=%async_computation.1 | async-start | bytes 65536 | tf_op jit(solution)/shard_map/all_to_all | solution.py:122
  103.2 15.5 %all-to-all-start = ((f32[100,16,128]{2,1,0:T(8,128)}), f32[100,16,128]{2,1,0:T(8,128)S(1)}, u32[]{:S(2)}, u32[]{:S(2)}) async-start(f32[100,16,128]{2,1,0:T(8,128)} %copy.69), calls=%async_computation | async-start | bytes 1638400 | tf_op jit(solution)/shard_map/all_to_all | solution.py:116
  (1 other events, 0.6 us)
